TPU v7x, 32 devices: a whole 2x2x4 slice. The times are simulated.
32 devices in a mesh: groups: 2 (over y), tensor: 4 (over z), section: 2 (over x), pool: 2 (over core).
Axes of the slice: x: 2, y: 2, z: 4, core: 2. Of those that a mesh axis runs over, the one named last changes fastest.
Arguments:
- cotangent: bfloat16 [6, 256, 8192], P('groups', None, ('tensor', 'pool')), parts along dimension 0, may hold values from -6 to 6
- saved_inputs: bfloat16 [2, 6, 256, 8192], P('section', 'groups', None, ('tensor', 'pool')), parts along dimension 1, may hold values from -6 to 6
- base_weight: bfloat16 [2, 8192, 4, 2, 1024], P('section', 'tensor', None, 'pool'), may hold values from -0.0625 to 0.0625
- panel_a: bfloat16 [2, 16, 64, 8192], P('section', 'pool', None, 'tensor'), may hold values from -0.0625 to 0.0625
- panel_b: bfloat16 [2, 16, 64, 8192], P('section', 'pool', None, 'tensor'), may hold values from -0.75 to 0.75
- seg_tiles: int32 [8], P('groups'), parts along dimension 0, may hold values from 1 to 2, 6 in all
- seg_adapter: int32 [8], P('groups'), parts along dimension 0, may hold values from 0 to 15
- slot_of: int32 [16], replicated, may hold values from 0 to 15, each once
Outputs:
- grad_inputs: bfloat16 [2, 6, 256, 8192], P('section', 'groups', None, ('tensor', 'pool')), parts along dimension 1
- grad_a: float32 [2, 32, 64, 8192], P('section', 'groups', None, ('tensor', 'pool')), parts along dimension 1
- grad_b: float32 [2, 32, 64, 8192], P('section', 'groups', None, ('tensor', 'pool')), parts along dimension 1
There are 2 independent parts, one for each index of `groups`. A program takes and returns all parts, laid end to end along the dimension named above; an argument that names none is the same for every part. Nothing has to cross between parts.
Inputs may be any that keep to these rules, and one draw needn't show every extreme that they name: `seg_tiles`: two segments cover 2 tiles each, all others 1, and the segments cover all 6 tiles. `slot_of`: each slot holds one adapter.
All inputs are finite; a program needn't handle non-finite values.
Results may differ from a plain program's by a relative error of at most 0.0048.
Values may be sent and summed in bfloat16 or wider, within the bound.
A program may use at most 192 MiB of HBM per device.

v0:
```python
import jax
import jax.numpy as jnp
from jax import lax
from jax.sharding import PartitionSpec as P

TILE = 128
TILES = 6
SEGS = 4


adapter_scale = 0.5


def passed_along(array, axis, by):
    size = lax.axis_size(axis)
    pairs = [(i, i + by) for i in range(size) if 0 <= i + by < size]
    return lax.ppermute(array, axis, pairs)


def tile_owners(seg_tiles, seg_adapter):
    ends = jnp.cumsum(seg_tiles)
    places = jnp.arange(TILES, dtype=jnp.int32)
    segment = jnp.sum((ends[None, :] <= places[:, None]).astype(jnp.int32), axis=1)
    picks = segment[:, None] == jnp.arange(SEGS, dtype=jnp.int32)[None, :]
    return jnp.sum(jnp.where(picks, seg_adapter[None, :], 0), axis=1)


def per_device(
    cotangent, saved_inputs, base_weight, panel_a, panel_b, seg_tiles, seg_adapter, slot_of
):
    sections = lax.axis_size("section")
    section_id = lax.axis_index("section")
    pool_id = lax.axis_index("pool")
    micro, row_count, narrow_rows = cotangent.shape
    per_micro = row_count // TILE
    weight = base_weight[0].reshape(base_weight.shape[1], -1)
    tile_adapter = tile_owners(seg_tiles, seg_adapter)
    matches = tile_adapter[:, None] == jnp.arange(slot_of.shape[0], dtype=jnp.int32)[None, :]
    tile_slot = jnp.sum(jnp.where(matches, slot_of[None, :], 0), axis=1)
    chooser = matches.astype(jnp.float32)
    every_a, every_b = (
        lax.all_gather(panel_a[0], "pool", axis=0, tiled=True),
        lax.all_gather(panel_b[0], "pool", axis=0, tiled=True),
    )
    tile_a = jnp.take(every_a, tile_slot, axis=0)
    tile_b = jnp.take(every_b, tile_slot, axis=0)
    tile_a = lax.dynamic_slice_in_dim(tile_a, pool_id * narrow_rows, narrow_rows, 2)
    tile_b = lax.dynamic_slice_in_dim(tile_b, pool_id * narrow_rows, narrow_rows, 2)
    spread_b = tile_b
    top = sections - 1
    ticks = micro + sections - 1

    def tick(step, carry):
        incoming, grad_inputs, grad_a, grad_b = carry
        index = step - (top - section_id)
        valid = (index >= 0) & (index < micro)
        which = jnp.clip(index, 0, micro - 1)
        first = lax.dynamic_index_in_dim(cotangent, which, 0, keepdims=False)
        own = jnp.where(section_id == top, first, incoming)
        inputs = lax.dynamic_index_in_dim(saved_inputs[0], which, 0, keepdims=False)
        panels_a = lax.dynamic_slice_in_dim(tile_a, which * per_micro, per_micro, 0)
        chosen = lax.dynamic_slice_in_dim(chooser, which * per_micro, per_micro, 0) * valid.astype(
            jnp.float32
        )
        gathered = lax.all_gather(own, "tensor", axis=1, tiled=True)
        partial_value = lax.dot_general(
            gathered, weight, (((1,), (1,)), ((), ())), preferred_element_type=jnp.float32
        )
        base_matrix = lax.psum_scatter(partial_value, "pool", scatter_dimension=1, tiled=True)
        gradient_cube3 = own.reshape(per_micro, TILE, narrow_rows)
        input_cube3 = inputs.reshape(per_micro, TILE, narrow_rows)
        shrink_in = jnp.einsum(
            "tkd,trd->tkr", input_cube3, panels_a, preferred_element_type=jnp.float32
        )
        panels_b = lax.dynamic_slice_in_dim(spread_b, which * per_micro, per_micro, 0)
        shrink_out = jnp.einsum(
            "tkd,trd->tkr", gradient_cube3, panels_b, preferred_element_type=jnp.float32
        )
        total_in, total_out = lax.psum((shrink_in, shrink_out), ("tensor", "pool"))
        lowrank_input = total_in.astype(jnp.bfloat16)
        lowrank_output = total_out.astype(jnp.bfloat16)
        expand_rows = jnp.einsum(
            "tkr,trd->tkd", lowrank_output, panels_a, preferred_element_type=jnp.float32
        )
        backward_result = (
            base_matrix + adapter_scale * expand_rows.reshape(row_count, narrow_rows)
        ).astype(jnp.bfloat16)
        update_first = adapter_scale * jnp.einsum(
            "fcj,fcm->fjm", lowrank_output, input_cube3, preferred_element_type=jnp.float32
        )
        update_second = adapter_scale * jnp.einsum(
            "fcj,fcm->fjm", lowrank_input, gradient_cube3, preferred_element_type=jnp.float32
        )
        grad_a = grad_a + jnp.einsum(
            "ta,trd->ard", chosen, update_first, precision=lax.Precision.HIGHEST
        )
        grad_b = grad_b + jnp.einsum(
            "ta,trd->ard", chosen, update_second, precision=lax.Precision.HIGHEST
        )
        current = lax.dynamic_index_in_dim(grad_inputs, which, 0, keepdims=False)
        grad_inputs = lax.dynamic_update_index_in_dim(
            grad_inputs, jnp.where(valid, backward_result, current), which, 0
        )
        outgoing = passed_along(backward_result, "section", -1)
        return (outgoing, grad_inputs, grad_a, grad_b)

    adapters = slot_of.shape[0]
    start = (
        jnp.zeros((row_count, narrow_rows), jnp.bfloat16),
        jnp.zeros((micro, row_count, narrow_rows), jnp.bfloat16),
        jnp.zeros((adapters, panel_a.shape[2], narrow_rows), jnp.float32),
        jnp.zeros((adapters, panel_a.shape[2], narrow_rows), jnp.float32),
    )
    last, grad_inputs, grad_a, grad_b = lax.fori_loop(0, ticks, tick, start)
    return (grad_inputs[None], grad_a[None], grad_b[None])


def solution(mesh):
    placed = (
        P("groups", None, ("tensor", "pool")),
        P("section", "groups", None, ("tensor", "pool")),
        P("section", "tensor", None, "pool", None),
        P("section", "pool", None, "tensor"),
        P("section", "pool", None, "tensor"),
        P("groups"),
        P("groups"),
        P(),
    )
    return jax.shard_map(
        per_device,
        mesh=mesh,
        in_specs=placed,
        out_specs=(
            P("section", "groups", None, ("tensor", "pool")),
            P("section", "groups", None, ("tensor", "pool")),
            P("section", "groups", None, ("tensor", "pool")),
        ),
        check_vma=False,
    )
```

profile of v0, /device:TPU:0, one launch (start us, length us, event | category | flops | bytes accessed | tf_op | source)
XLA Modules:
  0.0 529.5 jit_solution(7629185312404551196)
XLA Ops:
  8.9 17.5 %copy.23 = bf16[256,8,4,1024]{3,1,2,0:T(8,128)(2,1)} copy(bf16[256,8,4,1024]{3,2,1,0:T(4,128)(2,1)} %bitcast.78) | data formatting | bytes 33554432
  26.9 2.8 gather_fusion.1
  29.7 12.7 %all-gather.6.cloned.1.call-done = bf16[1,16,64,2048]{3,2,0,1:T(8,128)(2,1)} async-done(((bf16[1,8,64,2048]{3,2,0,1:T(8,128)(2,1)}), bf16[1,16,64,2048]{3,2,0,1:T(8,128)(2,1)}) %all-gather.6.cloned.1.call-update) | async-done | bytes 4194320 | tf_op jit(solution)/shard_map/all_gather | solution.py:43
  42.4 4.0 gather_fusion
  46.4 2.6 dynamic-slice_select_fusion
  50.4 460.5 %while.22 = (s32[]{:T(128)}, bf16[256,1024]{1,0:T(8,128)(2,1)S(1)}, bf16[3,256,1024]{2,1,0:T(8,128)(2,1)}, f32[16,64,1024]{2,0,1:T(8,128)}, f32[16,64,1024]{2,0,...) while((s32[]{:T(128)}, bf16[256,1024]{1,0:T(8,128)(2,1)S(1)}, ...), condition=%wide.region_8.10_spmd.clone, body=%wide.region_4.9_spmd.clone.sunk | while | flops 4518871040 | bytes 73042392 | solution.py:114
  52.4 47.6 %all-gather.10.cloned.1.call-done = bf16[256,4096]{1,0:T(8,128)(2,1)} async-done(((bf16[256,1024]{1,0:T(8,128)(2,1)}), bf16[256,4096]{1,0:T(8,128)(2,1)}) %all-gather.10.cloned.1.call-update) | async-done | bytes 2097168 | tf_op jit(solution)/shard_map/while/body/eval_jaxpr/all_gather | solution.py:65
  100.0 12.3 %fusion.64 = f32[256,2048]{1,0:T(8,128)} fusion(bf16[256,4096]{1,0:T(8,128)(2,1)} %all-gather.10.cloned.1.call-done, bf16[2048,4096]{1,0:T(8,128)(2,1)} %get-tuple-element.496), kind=kOutput, calls=%fused_computation.44.clone.1 | convolution fusion | flops 4294967296 | bytes 20971520 | tf_op jit(solution)/shard_map/while/body/eval_jaxpr/dot_general | solution.py:66
  115.0 28.0 %all-reduce.4 = (bf16[2,128,64]{1,2,0:T(8,128)(2,1)S(1)}, bf16[2,128,64]{1,2,0:T(8,128)(2,1)S(1)}) all-reduce(f32[2,128,64]{1,2,0:T(8,128)S(1)} %fusion.65, f32[2,128,64]{1,2,0:T(8,128)S(1)} %fusion.66), channel_id=1, replica_groups=mesh['groups'=2,'tensor'=4,'section'=2,'pool'=2] {'tensor','pool'}, use_global_device_ids=true, to_apply=%region_6.7 | all-reduce | flops 32768 | bytes 196608 | tf_op jit(solution)/shard_map/while/body/eval_jaxpr/psum | solution.py:79
  144.6 5.3 %select_add_fusion.4 = f32[16,64,1024]{2,0,1:T(8,128)} fusion(f32[16,64,1024]{2,0,1:T(8,128)} %get-tuple-element.473, pred[]{:T(512)S(6)} %compare.3, f32[2,64,1024]{2,1,0:T(8,128)S(1)} %convolution_multiply_fusion.7, f32[6,16]{1,0:T(8,128)S(1)} %get-tuple-element.499, s32[]{:T(128)S(6)} %select_n.112, f32[]{:T(128)S(6)} %convert_element_type.58), kind=kOutput, calls=%fused_computation.3.clone.1 | convolution fusion | flops 27263008 | bytes 8913929 | tf_op jit(solution)/shard_map/while/body/eval_jaxpr/ta,trd->ard/dot_general | solution.py:94
  153.9 5.3 %select_add_fusion.5 = f32[16,64,1024]{2,0,1:T(8,128)} fusion(f32[16,64,1024]{2,0,1:T(8,128)} %get-tuple-element.474, pred[]{:T(512)S(6)} %compare.3, f32[2,64,1024]{2,1,0:T(8,128)S(1)} %convolution_multiply_fusion.8, f32[6,16]{1,0:T(8,128)S(1)} %get-tuple-element.499, s32[]{:T(128)S(6)} %select_n.112, f32[]{:T(128)S(6)} %convert_element_type.58), kind=kOutput, calls=%fused_computation.2.clone.1 | convolution fusion | flops 27263008 | bytes 8913929 | tf_op jit(solution)/shard_map/while/body/eval_jaxpr/ta,trd->ard/dot_general | solution.py:97
  159.2 5.5 %collective-permute-done = bf16[256,1024]{1,0:T(8,128)(2,1)S(1)} collective-permute-done((bf16[256,1024]{1,0:T(8,128)(2,1)}, bf16[256,1024]{1,0:T(8,128)(2,1)S(1)}, u32[]{:S(2)}, u32[]{:S(2)}) %collective-permute-start) | collective-permute-done | bytes 524320 | tf_op jit(solution)/shard_map/while/body/eval_jaxpr/ppermute | solution.py:17
  166.7 46.9 %all-gather.10.cloned.1.call-done = bf16[256,4096]{1,0:T(8,128)(2,1)} async-done(((bf16[256,1024]{1,0:T(8,128)(2,1)}), bf16[256,4096]{1,0:T(8,128)(2,1)}) %all-gather.10.cloned.1.call-update) | async-done | bytes 2097168 | tf_op jit(solution)/shard_map/while/body/eval_jaxpr/all_gather | solution.py:65
  213.6 12.3 %fusion.64 = f32[256,2048]{1,0:T(8,128)} fusion(bf16[256,4096]{1,0:T(8,128)(2,1)} %all-gather.10.cloned.1.call-done, bf16[2048,4096]{1,0:T(8,128)(2,1)} %get-tuple-element.496), kind=kOutput, calls=%fused_computation.44.clone.1 | convolution fusion | flops 4294967296 | bytes 20971520 | tf_op jit(solution)/shard_map/while/body/eval_jaxpr/dot_general | solution.py:66
  228.6 28.0 %all-reduce.4 = (bf16[2,128,64]{1,2,0:T(8,128)(2,1)S(1)}, bf16[2,128,64]{1,2,0:T(8,128)(2,1)S(1)}) all-reduce(f32[2,128,64]{1,2,0:T(8,128)S(1)} %fusion.65, f32[2,128,64]{1,2,0:T(8,128)S(1)} %fusion.66), channel_id=1, replica_groups=mesh['groups'=2,'tensor'=4,'section'=2,'pool'=2] {'tensor','pool'}, use_global_device_ids=true, to_apply=%region_6.7 | all-reduce | flops 32768 | bytes 196608 | tf_op jit(solution)/shard_map/while/body/eval_jaxpr/psum | solution.py:79
  258.3 6.9 %select_add_fusion.4 = f32[16,64,1024]{2,0,1:T(8,128)} fusion(f32[16,64,1024]{2,0,1:T(8,128)} %get-tuple-element.473, pred[]{:T(512)S(6)} %compare.3, f32[2,64,1024]{2,1,0:T(8,128)S(1)} %convolution_multiply_fusion.7, f32[6,16]{1,0:T(8,128)S(1)} %get-tuple-element.499, s32[]{:T(128)S(6)} %select_n.112, f32[]{:T(128)S(6)} %convert_element_type.58), kind=kOutput, calls=%fused_computation.3.clone.1 | convolution fusion | flops 27263008 | bytes 8913929 | tf_op jit(solution)/shard_map/while/body/eval_jaxpr/ta,trd->ard/dot_general | solution.py:94
  269.1 6.9 %select_add_fusion.5 = f32[16,64,1024]{2,0,1:T(8,128)} fusion(f32[16,64,1024]{2,0,1:T(8,128)} %get-tuple-element.474, pred[]{:T(512)S(6)} %compare.3, f32[2,64,1024]{2,1,0:T(8,128)S(1)} %convolution_multiply_fusion.8, f32[6,16]{1,0:T(8,128)S(1)} %get-tuple-element.499, s32[]{:T(128)S(6)} %select_n.112, f32[]{:T(128)S(6)} %convert_element_type.58), kind=kOutput, calls=%fused_computation.2.clone.1 | convolution fusion | flops 27263008 | bytes 8913929 | tf_op jit(solution)/shard_map/while/body/eval_jaxpr/ta,trd->ard/dot_general | solution.py:97
  276.0 4.0 collective-permute-done
  281.9 47.2 %all-gather.10.cloned.1.call-done = bf16[256,4096]{1,0:T(8,128)(2,1)} async-done(((bf16[256,1024]{1,0:T(8,128)(2,1)}), bf16[256,4096]{1,0:T(8,128)(2,1)}) %all-gather.10.cloned.1.call-update) | async-done | bytes 2097168 | tf_op jit(solution)/shard_map/while/body/eval_jaxpr/all_gather | solution.py:65
  329.1 12.3 %fusion.64 = f32[256,2048]{1,0:T(8,128)} fusion(bf16[256,4096]{1,0:T(8,128)(2,1)} %all-gather.10.cloned.1.call-done, bf16[2048,4096]{1,0:T(8,128)(2,1)} %get-tuple-element.496), kind=kOutput, calls=%fused_computation.44.clone.1 | convolution fusion | flops 4294967296 | bytes 20971520 | tf_op jit(solution)/shard_map/while/body/eval_jaxpr/dot_general | solution.py:66
  344.1 28.0 %all-reduce.4 = (bf16[2,128,64]{1,2,0:T(8,128)(2,1)S(1)}, bf16[2,128,64]{1,2,0:T(8,128)(2,1)S(1)}) all-reduce(f32[2,128,64]{1,2,0:T(8,128)S(1)} %fusion.65, f32[2,128,64]{1,2,0:T(8,128)S(1)} %fusion.66), channel_id=1, replica_groups=mesh['groups'=2,'tensor'=4,'section'=2,'pool'=2] {'tensor','pool'}, use_global_device_ids=true, to_apply=%region_6.7 | all-reduce | flops 32768 | bytes 196608 | tf_op jit(solution)/shard_map/while/body/eval_jaxpr/psum | solution.py:79
  373.8 6.9 %select_add_fusion.4 = f32[16,64,1024]{2,0,1:T(8,128)} fusion(f32[16,64,1024]{2,0,1:T(8,128)} %get-tuple-element.473, pred[]{:T(512)S(6)} %compare.3, f32[2,64,1024]{2,1,0:T(8,128)S(1)} %convolution_multiply_fusion.7, f32[6,16]{1,0:T(8,128)S(1)} %get-tuple-element.499, s32[]{:T(128)S(6)} %select_n.112, f32[]{:T(128)S(6)} %convert_element_type.58), kind=kOutput, calls=%fused_computation.3.clone.1 | convolution fusion | flops 27263008 | bytes 8913929 | tf_op jit(solution)/shard_map/while/body/eval_jaxpr/ta,trd->ard/dot_general | solution.py:94
  380.6 2.5 bitcast_dynamic-update-slice_fusion.2
  384.6 6.9 %select_add_fusion.5 = f32[16,64,1024]{2,0,1:T(8,128)} fusion(f32[16,64,1024]{2,0,1:T(8,128)} %get-tuple-element.474, pred[]{:T(512)S(6)} %compare.3, f32[2,64,1024]{2,1,0:T(8,128)S(1)} %convolution_multiply_fusion.8, f32[6,16]{1,0:T(8,128)S(1)} %get-tuple-element.499, s32[]{:T(128)S(6)} %select_n.112, f32[]{:T(128)S(6)} %convert_element_type.58), kind=kOutput, calls=%fused_computation.2.clone.1 | convolution fusion | flops 27263008 | bytes 8913929 | tf_op jit(solution)/shard_map/while/body/eval_jaxpr/ta,trd->ard/dot_general | solution.py:97
  391.5 4.0 collective-permute-done
  397.4 47.1 %all-gather.10.cloned.1.call-done = bf16[256,4096]{1,0:T(8,128)(2,1)} async-done(((bf16[256,1024]{1,0:T(8,128)(2,1)}), bf16[256,4096]{1,0:T(8,128)(2,1)}) %all-gather.10.cloned.1.call-update) | async-done | bytes 2097168 | tf_op jit(solution)/shard_map/while/body/eval_jaxpr/all_gather | solution.py:65
  444.6 12.3 %fusion.64 = f32[256,2048]{1,0:T(8,128)} fusion(bf16[256,4096]{1,0:T(8,128)(2,1)} %all-gather.10.cloned.1.call-done, bf16[2048,4096]{1,0:T(8,128)(2,1)} %get-tuple-element.496), kind=kOutput, calls=%fused_computation.44.clone.1 | convolution fusion | flops 4294967296 | bytes 20971520 | tf_op jit(solution)/shard_map/while/body/eval_jaxpr/dot_general | solution.py:66
  459.6 28.0 %all-reduce.4 = (bf16[2,128,64]{1,2,0:T(8,128)(2,1)S(1)}, bf16[2,128,64]{1,2,0:T(8,128)(2,1)S(1)}) all-reduce(f32[2,128,64]{1,2,0:T(8,128)S(1)} %fusion.65, f32[2,128,64]{1,2,0:T(8,128)S(1)} %fusion.66), channel_id=1, replica_groups=mesh['groups'=2,'tensor'=4,'section'=2,'pool'=2] {'tensor','pool'}, use_global_device_ids=true, to_apply=%region_6.7 | all-reduce | flops 32768 | bytes 196608 | tf_op jit(solution)/shard_map/while/body/eval_jaxpr/psum | solution.py:79
  489.3 6.9 %select_add_fusion.4 = f32[16,64,1024]{2,0,1:T(8,128)} fusion(f32[16,64,1024]{2,0,1:T(8,128)} %get-tuple-element.473, pred[]{:T(512)S(6)} %compare.3, f32[2,64,1024]{2,1,0:T(8,128)S(1)} %convolution_multiply_fusion.7, f32[6,16]{1,0:T(8,128)S(1)} %get-tuple-element.499, s32[]{:T(128)S(6)} %select_n.112, f32[]{:T(128)S(6)} %convert_element_type.58), kind=kOutput, calls=%fused_computation.3.clone.1 | convolution fusion | flops 27263008 | bytes 8913929 | tf_op jit(solution)/shard_map/while/body/eval_jaxpr/ta,trd->ard/dot_general | solution.py:94
  500.1 6.9 %select_add_fusion.5 = f32[16,64,1024]{2,0,1:T(8,128)} fusion(f32[16,64,1024]{2,0,1:T(8,128)} %get-tuple-element.474, pred[]{:T(512)S(6)} %compare.3, f32[2,64,1024]{2,1,0:T(8,128)S(1)} %convolution_multiply_fusion.8, f32[6,16]{1,0:T(8,128)S(1)} %get-tuple-element.499, s32[]{:T(128)S(6)} %select_n.112, f32[]{:T(128)S(6)} %convert_element_type.58), kind=kOutput, calls=%fused_computation.2.clone.1 | convolution fusion | flops 27263008 | bytes 8913929 | tf_op jit(solution)/shard_map/while/body/eval_jaxpr/ta,trd->ard/dot_general | solution.py:97
  507.0 4.0 collective-permute-done
  510.9 11.7 %copy_bitcast_fusion = (f32[1,16,64,1024]{3,2,1,0:T(8,128)}, f32[1,16,64,1024]{3,2,1,0:T(8,128)}) fusion(f32[16,64,1024]{2,0,1:T(8,128)} %get-tuple-element.288, f32[16,64,1024]{2,0,1:T(8,128)} %get-tuple-element.287), kind=kLoop, calls=%fused_computation.30 | loop fusion | bytes 16777216 | tf_op jit(solution)/shard_map/broadcast_in_dim | solution.py:115
  (90 shorter events, 41.9 us)
Async XLA Ops:
  7.2 1.5 copy-start.1
  7.2 19.7 %all-gather.8.cloned.1.call-start = ((), (), s32[]{:S(2)}) async-start(), calls=%async_computation.2 | async-start | bytes 6291456 | tf_op jit(solution)/shard_map/all_gather | solution.py:42
  7.9 34.5 %all-gather.6.cloned.1.call-start = ((), (), s32[]{:S(2)}) async-start(), calls=%async_computation.1 | async-start | bytes 6291456 | tf_op jit(solution)/shard_map/all_gather | solution.py:43
  8.9 17.6 %copy-start.2 = (s32[4]{0:T(128)S(1)}, s32[4]{0:T(128)}, u32[]{:S(2)}) copy-start(s32[4]{0:T(128)} %param.18) | copy-start | bytes 52
  8.9 17.7 %copy-start.3 = (s32[16]{0:T(128)S(1)}, s32[16]{0:T(128)}, u32[]{:S(2)}) copy-start(s32[16]{0:T(128)} %param.19) | copy-start | bytes 196
  50.4 49.5 %all-gather.10.cloned.1.call-start = ((), (), s32[]{:S(2)}) async-start(), calls=%async_computation.3 | async-start | bytes 2621440 | tf_op jit(solution)/shard_map/while/body/eval_jaxpr/all_gather | solution.py:65
  52.3 97.6 %reduce-scatter.2.cloned.1.call-start = ((), (), s32[]{:S(2)}) async-start(), calls=%async_computation.4 | async-start | bytes 3145728 | tf_op jit(solution)/shard_map/while/body/eval_jaxpr/reduce_scatter | solution.py:69
  100.0 12.3 %copy-start = (bf16[256,1024]{1,0:T(8,128)(2,1)S(1)}, bf16[256,1024]{1,0:T(8,128)(2,1)}, u32[]{:S(2)}) copy-start(bf16[256,1024]{1,0:T(8,128)(2,1)} %bitcast_select_fusion.3) | copy-start | bytes 1572868 | tf_op jit(solution)/shard_map/while
  152.4 12.3 %collective-permute-start = (bf16[256,1024]{1,0:T(8,128)(2,1)}, bf16[256,1024]{1,0:T(8,128)(2,1)S(1)}, u32[]{:S(2)}, u32[]{:S(2)}) collective-permute-start(bf16[256,1024]{1,0:T(8,128)(2,1)} %get-tuple-element.449), channel_id=1, source_target_pairs={{2,0},{3,1},{6,4},{7,5},{10,8},{11,9},{14,12},{15,13},{18,16},{19,... | collective-permute-start | bytes 1572872 | tf_op jit(solution)/shard_map/while/body/eval_jaxpr/ppermute | solution.py:17
  164.8 48.8 %all-gather.10.cloned.1.call-start = ((), (), s32[]{:S(2)}) async-start(), calls=%async_computation.3 | async-start | bytes 2621440 | tf_op jit(solution)/shard_map/while/body/eval_jaxpr/all_gather | solution.py:65
  166.7 98.5 %reduce-scatter.2.cloned.1.call-start = ((), (), s32[]{:S(2)}) async-start(), calls=%async_computation.4 | async-start | bytes 3145728 | tf_op jit(solution)/shard_map/while/body/eval_jaxpr/reduce_scatter | solution.py:69
  213.6 12.3 %copy-start = (bf16[256,1024]{1,0:T(8,128)(2,1)S(1)}, bf16[256,1024]{1,0:T(8,128)(2,1)}, u32[]{:S(2)}) copy-start(bf16[256,1024]{1,0:T(8,128)(2,1)} %bitcast_select_fusion.3) | copy-start | bytes 1572868 | tf_op jit(solution)/shard_map/while
  267.6 12.3 %collective-permute-start = (bf16[256,1024]{1,0:T(8,128)(2,1)}, bf16[256,1024]{1,0:T(8,128)(2,1)S(1)}, u32[]{:S(2)}, u32[]{:S(2)}) collective-permute-start(bf16[256,1024]{1,0:T(8,128)(2,1)} %get-tuple-element.449), channel_id=1, source_target_pairs={{2,0},{3,1},{6,4},{7,5},{10,8},{11,9},{14,12},{15,13},{18,16},{19,... | collective-permute-start | bytes 1572872 | tf_op jit(solution)/shard_map/while/body/eval_jaxpr/ppermute | solution.py:17
  279.9 49.1 %all-gather.10.cloned.1.call-start = ((), (), s32[]{:S(2)}) async-start(), calls=%async_computation.3 | async-start | bytes 2621440 | tf_op jit(solution)/shard_map/while/body/eval_jaxpr/all_gather | solution.py:65
  281.9 98.8 %reduce-scatter.2.cloned.1.call-start = ((), (), s32[]{:S(2)}) async-start(), calls=%async_computation.4 | async-start | bytes 3145728 | tf_op jit(solution)/shard_map/while/body/eval_jaxpr/reduce_scatter | solution.py:69
  329.1 12.3 %copy-start = (bf16[256,1024]{1,0:T(8,128)(2,1)S(1)}, bf16[256,1024]{1,0:T(8,128)(2,1)}, u32[]{:S(2)}) copy-start(bf16[256,1024]{1,0:T(8,128)(2,1)} %bitcast_select_fusion.3) | copy-start | bytes 1572868 | tf_op jit(solution)/shard_map/while
  383.1 12.3 %collective-permute-start = (bf16[256,1024]{1,0:T(8,128)(2,1)}, bf16[256,1024]{1,0:T(8,128)(2,1)S(1)}, u32[]{:S(2)}, u32[]{:S(2)}) collective-permute-start(bf16[256,1024]{1,0:T(8,128)(2,1)} %get-tuple-element.449), channel_id=1, source_target_pairs={{2,0},{3,1},{6,4},{7,5},{10,8},{11,9},{14,12},{15,13},{18,16},{19,... | collective-permute-start | bytes 1572872 | tf_op jit(solution)/shard_map/while/body/eval_jaxpr/ppermute | solution.py:17
  395.4 49.1 %all-gather.10.cloned.1.call-start = ((), (), s32[]{:S(2)}) async-start(), calls=%async_computation.3 | async-start | bytes 2621440 | tf_op jit(solution)/shard_map/while/body/eval_jaxpr/all_gather | solution.py:65
  397.4 98.8 %reduce-scatter.2.cloned.1.call-start = ((), (), s32[]{:S(2)}) async-start(), calls=%async_computation.4 | async-start | bytes 3145728 | tf_op jit(solution)/shard_map/while/body/eval_jaxpr/reduce_scatter | solution.py:69
  444.6 12.3 %copy-start = (bf16[256,1024]{1,0:T(8,128)(2,1)S(1)}, bf16[256,1024]{1,0:T(8,128)(2,1)}, u32[]{:S(2)}) copy-start(bf16[256,1024]{1,0:T(8,128)(2,1)} %bitcast_select_fusion.3) | copy-start | bytes 1572868 | tf_op jit(solution)/shard_map/while
  498.6 12.3 %collective-permute-start = (bf16[256,1024]{1,0:T(8,128)(2,1)}, bf16[256,1024]{1,0:T(8,128)(2,1)S(1)}, u32[]{:S(2)}, u32[]{:S(2)}) collective-permute-start(bf16[256,1024]{1,0:T(8,128)(2,1)} %get-tuple-element.449), channel_id=1, source_target_pairs={{2,0},{3,1},{6,4},{7,5},{10,8},{11,9},{14,12},{15,13},{18,16},{19,... | collective-permute-start | bytes 1572872 | tf_op jit(solution)/shard_map/while/body/eval_jaxpr/ppermute | solution.py:17
Sparse Core Ops, SparseCore 0:
  9.6 16.3 all-gather.7
  27.5 14.8 all-gather.5
  52.8 47.0 all-gather.9
  112.4 8.3 reduce-scatter.1
  166.8 46.6 all-gather.9
  226.0 8.3 reduce-scatter.1
  282.3 46.6 all-gather.9
  341.5 8.3 reduce-scatter.1
  397.8 46.6 all-gather.9
  457.0 8.3 reduce-scatter.1
where the time goes:
time: 531 us; the launch traced here: 529 us
  waiting for transfers between devices  220 us (41%)
  blocking collectives  112 us (21%)
  matrix products  110 us (21%)
  local copies, waits for them, and re-layouts  46.2 us (9%)
  other arithmetic  20.7 us (4%)
  between operations  14.1 us (3%)
  starting transfers between devices  5.38 us (1%)
    all_gather x4, waiting for transfers between devices, tick(): gathered = lax.all_gather(own, 'tensor', axis=1, tiled=True)  189 us
    psum x4, blocking collectives, tick(): total_in, total_out = lax.psum((shrink_in, shrink_out), ('tensor', 'pool'))  112 us
    dot_general x4, matrix products, tick(): lax.dot_general(gathered, weight, (((1,), (1,)), ((), ())), preferred_ele...  49.2 us
    dot_general x4, matrix products, tick(): jnp.einsum('ta,trd->ard', chosen, update_second, precision=lax.Precision....  25.9 us
    dot_general x4, matrix products, tick(): jnp.einsum('ta,trd->ard', chosen, update_first, precision=lax.Precision.H...  25.9 us
    unnamed x7, local copies, waits for them, and re-layouts  17.6 us
    ppermute x4, waiting for transfers between devices, passed_along(): return lax.ppermute(array, axis, pairs)  17.4 us
    all_gather x1, waiting for transfers between devices, per_device(): lax.all_gather(panel_b[0], 'pool', axis=0, tiled=True)  12.7 us
  transfers between devices with their start and end apart: 14, of which 9 were waited for; matrix products, arithmetic and copies ran while one was open for 17% of the time, Pallas kernels for 0%

commit v1 on v0

v1 whole, which is shorter than its diff:
```python
import jax
import jax.numpy as jnp
from jax import lax
from jax.experimental import pallas as pl
from jax.experimental.pallas import tpu as pltpu
from jax.sharding import PartitionSpec as P

TILE = 128
SCALE = 0.5
AHEAD = 2
MESH = pl.DeviceIdType.MESH
F32 = jnp.float32
BF16 = jnp.bfloat16


def tile_owners(seg_tiles, seg_adapter, tiles):
    segs = seg_tiles.shape[0]
    ends = jnp.cumsum(seg_tiles)
    places = jnp.arange(tiles, dtype=jnp.int32)
    segment = jnp.sum((ends[None, :] <= places[:, None]).astype(jnp.int32), axis=1)
    picks = segment[:, None] == jnp.arange(segs, dtype=jnp.int32)[None, :]
    return jnp.sum(jnp.where(picks, seg_adapter[None, :], 0), axis=1)


def row_dot(a, b):
    return lax.dot_general(a, b, (((1,), (1,)), ((), ())), preferred_element_type=F32)


def kernel(
    seg_tiles, seg_adapter, slot_of, cot, x, w_hbm, panel_a, panel_b,
    grad_in, grad_own, low_u, low_h,
    w, gath, part, part_in, own_acc, sel_a, sel_b, put_a, put_b,
    u_part, u_pool, u_sum, u_all, h_part, h_pool, h_sum, h_all,
    w_sem, g_send, g_recv, u_send, u_recv, up_send, up_recv, pp_send, pp_recv,
    sel_send, sel_recv, hp_send, hp_recv, h_send, h_recv, s_send, s_recv,
):
    n = lax.axis_size("tensor")
    top = lax.axis_size("section") - 1
    s, t, p = lax.axis_index("section"), lax.axis_index("tensor"), lax.axis_index("pool")
    q = 1 - p
    rows_all, width = cot.shape
    tiles = rows_all // TILE
    segs = seg_tiles.shape[0]
    slots = panel_a.shape[0]
    block = min(256, width)

    barrier = pltpu.get_barrier_semaphore()

    def greet(i, _):
        pl.semaphore_signal(barrier, inc=1, device_id={"tensor": lax.rem(t + i, n)}, device_id_type=MESH)
        return 0

    lax.fori_loop(1, n, greet, 0)
    pl.semaphore_signal(barrier, inc=1, device_id={"pool": q}, device_id_type=MESH)

    @pl.when(s > 0)
    def _():
        pl.semaphore_signal(barrier, inc=1, device_id={"section": s - 1}, device_id_type=MESH)

    @pl.when(s < top)
    def _():
        pl.semaphore_signal(barrier, inc=1, device_id={"section": s + 1}, device_id_type=MESH)

    w_copy = pltpu.make_async_copy(w_hbm, w, w_sem)
    w_copy.start()
    pl.semaphore_wait(barrier, n + (s > 0).astype(jnp.int32) + (s < top).astype(jnp.int32))

    def rows(k):
        return pl.ds(pl.multiple_of(k * TILE, TILE), TILE)

    def gather_copy(k, sender, target):
        place = gath.at[sender, rows(k)]
        return pltpu.make_async_remote_copy(
            place, place, g_send.at[k, target], g_recv.at[k, sender],
            device_id={"tensor": target}, device_id_type=MESH)

    def u_copy(k, sender, target):
        return pltpu.make_async_remote_copy(
            u_sum.at[k], u_all.at[k, sender], u_send.at[k, target], u_recv.at[k, sender],
            device_id={"tensor": target}, device_id_type=MESH)

    def h_copy(sender, target):
        return pltpu.make_async_remote_copy(
            h_sum, h_all.at[sender], h_send.at[target], h_recv.at[sender],
            device_id={"tensor": target}, device_id_type=MESH)

    def pool_copy(source, dest, send, recv):
        return pltpu.make_async_remote_copy(
            source, dest, send, recv, device_id={"pool": q}, device_id_type=MESH)

    def section_copy(k):
        return pltpu.make_async_remote_copy(
            grad_in.at[rows(k)], gath.at[t, rows(k)], s_send.at[k], s_recv.at[k],
            device_id={"section": jnp.maximum(s - 1, 0)}, device_id_type=MESH)

    def others(body):
        def run(i, _):
            body(lax.rem(t + i, n))
            return 0

        lax.fori_loop(1, n, run, 0)

    @pl.when(s == top)
    def _():
        gath[t] = cot[...]

        def first(k, _):
            others(lambda tt: gather_copy(k, t, tt).start())
            return 0

        lax.fori_loop(0, min(AHEAD, tiles), first, 0)

    mine = pl.ds(pl.multiple_of(p * width, width), width)
    theirs = pl.ds(pl.multiple_of(q * width, width), width)
    seg_slot = [slot_of[seg_adapter[j]] for j in range(segs)]
    for j in range(segs):
        local = jnp.clip(seg_slot[j] - p * slots, 0, slots - 1)
        put_b[j] = panel_b[local, :, theirs]
        sel_b[0, j] = panel_b[local, :, mine]
    copy_b = pool_copy(put_b, sel_b.at[1], sel_send.at[0], sel_recv.at[0])
    copy_b.start()
    for j in range(segs):
        local = jnp.clip(seg_slot[j] - p * slots, 0, slots - 1)
        put_a[j] = panel_a[local, :, theirs]
        sel_a[0, j] = panel_a[local, :, mine]
    copy_a = pool_copy(put_a, sel_a.at[1], sel_send.at[1], sel_recv.at[1])
    copy_a.start()
    copy_b.wait()
    copy_a.wait()

    def chosen(k, sel):
        total, segment = jnp.int32(0), jnp.int32(0)
        for j in range(segs - 1):
            total = total + seg_tiles[j]
            segment = segment + (total <= k).astype(jnp.int32)
        slot = slot_of[seg_adapter[segment]]
        home = (slot >= p * slots) & (slot < (p + 1) * slots)
        return sel[1 - home.astype(jnp.int32), segment]

    def launch(k):
        @pl.when(s < top)
        def _():
            section_copy(k).wait_recv()
            others(lambda tt: gather_copy(k, t, tt).start())

        u_part[k] = row_dot(chosen(k, sel_b), gath[t, rows(k)])
        pool_copy(u_part.at[k], u_pool.at[k], up_send.at[k], up_recv.at[k]).start()

    launch(0)

    def shrink_x(k, _):
        h_part[:, rows(k)] = row_dot(chosen(k, sel_a), x[rows(k)])
        return 0

    lax.fori_loop(0, tiles, shrink_x, 0)
    h_pool_copy = pool_copy(h_part, h_pool, hp_send, hp_recv)
    h_pool_copy.start()
    w_copy.wait()
    h_pool_copy.wait()
    h_sum[...] = h_part[...] + h_pool[...]
    others(lambda tt: h_copy(t, tt).start())

    def multiply(k, tt, half, acc, fresh):
        def one(b, _):
            r = pl.multiple_of(b * block, block)
            wr = pl.ds(pl.multiple_of(half * width + r, block), block)
            wc = pl.ds(pl.multiple_of(tt * width, width), width)
            product = row_dot(gath[tt, rows(k)], w[wr, wc])
            if fresh:
                acc[:, pl.ds(r, block)] = product
            else:
                acc[:, pl.ds(r, block)] += product
            return 0

        lax.fori_loop(0, width // block, one, 0)

    def process(k, _):
        @pl.when(k + 1 < tiles)
        def _():
            launch(k + 1)

        pool_copy(u_part.at[k], u_pool.at[k], up_send.at[k], up_recv.at[k]).wait()
        u_sum[k] = u_part[k] + u_pool[k]
        others(lambda tt: u_copy(k, t, tt).start())

        send = part.at[k]
        multiply(k, t, q, send, True)
        multiply(k, t, p, own_acc, True)

        def middle(i, _):
            tt = lax.rem(t + i, n)
            gather_copy(k, tt, tt).wait_recv()
            multiply(k, tt, q, send, False)
            multiply(k, tt, p, own_acc, False)
            return 0

        lax.fori_loop(1, n - 1, middle, 0)
        last = lax.rem(t + n - 1, n)
        gather_copy(k, last, last).wait_recv()

        @pl.when((s == top) & (k + AHEAD < tiles))
        def _():
            others(lambda tt: gather_copy(k + AHEAD, t, tt).start())

        multiply(k, last, q, send, False)
        half_copy = pool_copy(send, part_in.at[k], pp_send.at[k], pp_recv.at[k])
        half_copy.start()
        multiply(k, last, p, own_acc, False)
        u_all[k, t] = u_sum[k]
        others(lambda tt: u_copy(k, tt, tt).wait_recv())
        u = u_all[k, 0]
        for i in range(1, n):
            u = u + u_all[k, i]
        low_u[:, rows(k)] = u.astype(BF16)
        expand = jnp.dot(u.T.astype(BF16), chosen(k, sel_a), preferred_element_type=F32)
        half_copy.wait()
        grad_in[rows(k)] = (own_acc[...] + part_in[k] + SCALE * expand).astype(BF16)

        @pl.when(s > 0)
        def _():
            section_copy(k).start()

        return 0

    lax.fori_loop(0, tiles, process, 0)

    grad_own[...] = gath[t]
    h_all[t] = h_sum[...]
    others(lambda tt: h_copy(tt, tt).wait_recv())
    h = h_all[0]
    for i in range(1, n):
        h = h + h_all[i]
    low_h[...] = h.astype(BF16)

    def sent(tt):
        h_copy(t, tt).wait_send()

        def one(k, _):
            gather_copy(k, t, tt).wait_send()
            u_copy(k, t, tt).wait_send()
            return 0

        lax.fori_loop(0, tiles, one, 0)

    others(sent)

    @pl.when(s > 0)
    def _():
        def one(k, _):
            section_copy(k).wait_send()
            return 0

        lax.fori_loop(0, tiles, one, 0)


def per_device(cotangent, saved_inputs, base_weight, panel_a, panel_b, seg_tiles, seg_adapter, slot_of):
    n = lax.axis_size("tensor")
    micro, row_count, width = cotangent.shape
    m = micro * row_count
    tiles = m // TILE
    weight = base_weight[0].reshape(base_weight.shape[1], -1)
    x = saved_inputs[0].reshape(m, width)
    rank = panel_a.shape[2]
    segs = seg_tiles.shape[0]
    smem = pl.BlockSpec(memory_space=pltpu.SMEM)
    vmem = pl.BlockSpec(memory_space=pltpu.VMEM)
    dma = pltpu.SemaphoreType.DMA
    grad_in, grad_own, low_u, low_h = pl.pallas_call(
        kernel,
        out_shape=(
            jax.ShapeDtypeStruct((m, width), BF16),
            jax.ShapeDtypeStruct((m, width), BF16),
            jax.ShapeDtypeStruct((rank, m), BF16),
            jax.ShapeDtypeStruct((rank, m), BF16),
        ),
        in_specs=[smem] * 3 + [vmem] * 2 + [pl.BlockSpec(memory_space=pl.ANY)] + [vmem] * 2,
        out_specs=(vmem,) * 4,
        scratch_shapes=[
            pltpu.VMEM(weight.shape, BF16),
            pltpu.VMEM((n, m, width), BF16),
            pltpu.VMEM((tiles, TILE, width), F32),
            pltpu.VMEM((tiles, TILE, width), F32),
            pltpu.VMEM((TILE, width), F32),
            pltpu.VMEM((2, segs, rank, width), BF16),
            pltpu.VMEM((2, segs, rank, width), BF16),
            pltpu.VMEM((segs, rank, width), BF16),
            pltpu.VMEM((segs, rank, width), BF16),
            pltpu.VMEM((tiles, rank, TILE), F32),
            pltpu.VMEM((tiles, rank, TILE), F32),
            pltpu.VMEM((tiles, rank, TILE), F32),
            pltpu.VMEM((tiles, n, rank, TILE), F32),
            pltpu.VMEM((rank, m), F32),
            pltpu.VMEM((rank, m), F32),
            pltpu.VMEM((rank, m), F32),
            pltpu.VMEM((n, rank, m), F32),
            dma(()),
            dma((tiles, n)), dma((tiles, n)), dma((tiles, n)), dma((tiles, n)),
            dma((tiles,)), dma((tiles,)), dma((tiles,)), dma((tiles,)),
            dma((2,)), dma((2,)), dma(()), dma(()), dma((n,)), dma((n,)),
            dma((tiles,)), dma((tiles,)),
        ],
        compiler_params=pltpu.CompilerParams(
            collective_id=0, has_side_effects=True, vmem_limit_bytes=58 * 1024 * 1024),
    )(seg_tiles, seg_adapter, slot_of, cotangent.reshape(m, width), x, weight, panel_a[0], panel_b[0])

    adapters = slot_of.shape[0]
    owners = jnp.repeat(tile_owners(seg_tiles, seg_adapter, tiles), TILE)
    hit = owners[None, :] == jnp.arange(adapters, dtype=jnp.int32)[:, None]

    def spread(low, wide):
        lanes = jnp.where(hit[:, None, :], low[None], jnp.zeros((), BF16)).reshape(adapters * rank, m)
        full = SCALE * jnp.dot(lanes, wide, preferred_element_type=F32)
        return full.reshape(1, adapters, rank, width)

    return (grad_in.reshape(1, micro, row_count, width), spread(low_u, x), spread(low_h, grad_own))


def solution(mesh):
    placed = (
        P("groups", None, ("tensor", "pool")),
        P("section", "groups", None, ("tensor", "pool")),
        P("section", "tensor", None, "pool", None),
        P("section", "pool", None, "tensor"),
        P("section", "pool", None, "tensor"),
        P("groups"),
        P("groups"),
        P(),
    )
    out = P("section", "groups", None, ("tensor", "pool"))
    return jax.shard_map(
        per_device, mesh=mesh, in_specs=placed, out_specs=(out, out, out), check_vma=False)
```

time: 531 us -> 302 us (0.57)
  Pallas kernels: 0 us -> 273 us
  waiting for transfers between devices: 220 us -> 0 us
  blocking collectives: 112 us -> 0 us
  matrix products: 110 us -> 7.61 us
  local copies, waits for them, and re-layouts: 46.2 us -> 18.5 us
  other arithmetic: 20.7 us -> 1.64 us
  between operations: 14.1 us -> 0.67 us
  starting transfers between devices: 5.38 us -> 0 us
    pallas_call x0 -> x1, Pallas kernels: none -> 273 us  [per_device(): pl.pallas_call(kernel, out_shape=(jax.ShapeDtypeStruct((m, width), BF16),...]
    all_gather x6 -> x0, waiting for transfers between devices: 201 us -> none  [the longest x4 189 us: tick(): gathered = lax.all_gather(own, 'tensor', axis=1, tiled=True)]
    psum x4 -> x0, blocking collectives: 112 us -> none  [tick(): total_in, total_out = lax.psum((shrink_in, shrink_out), ('tensor', 'pool'))]
    dot_general x32 -> x2, matrix products: 110 us -> 7.61 us  [spread(): full = SCALE * jnp.dot(lanes, wide, preferred_element_type=F32)]
    ppermute x4 -> x0, waiting for transfers between devices: 17.4 us -> none  [passed_along(): return lax.ppermute(array, axis, pairs)]
    broadcast_in_dim x3 -> x0, local copies, waits for them, and re-layouts: 13.1 us -> none  [the longest x1 11.7 us: per_device(): return (grad_inputs[None], grad_a[None], grad_b[None])]
    dynamic_update_slice x4 -> x0, other arithmetic: 9.85 us -> none  [tick(): lax.dynamic_update_index_in_dim(grad_inputs, jnp.where(valid, backward_re...]
    select_n x6 -> x1, other arithmetic: 10.2 us -> 1.28 us  [spread(): jnp.where(hit[:, None, :], low[None], jnp.zeros((), BF16))]
  transfers between devices with their start and end apart: 14 -> 0, of which waited for: 9 -> 0; matrix products, arithmetic and copies ran while one was open for 17% -> 0% of each run, Pallas kernels for 0% -> 0%
where the time goes in v1:
time: 302 us; the launch traced here: 301 us
  Pallas kernels  273 us (90%)
  local copies, waits for them, and re-layouts  18.5 us (6%)
  matrix products  7.61 us (3%)
    pallas_call x1, Pallas kernels, per_device(): pl.pallas_call(kernel, out_shape=(jax.ShapeDtypeStruct((m, width), BF16),...  273 us
    unnamed x12, local copies, waits for them, and re-layouts  18.4 us
    dot_general x2, matrix products, spread(): full = SCALE * jnp.dot(lanes, wide, preferred_element_type=F32)  7.61 us

profile of v1, /device:TPU:0, one launch (start us, length us, event | category | flops | bytes accessed | tf_op | source)
XLA Modules:
  0.0 301.4 jit_solution(6440836077348785472)
XLA Ops:
  0.6 17.0 %copy.11 = bf16[256,8,4,1024]{3,1,2,0:T(8,128)(2,1)} copy(bf16[256,8,4,1024]{3,2,1,0:T(4,128)(2,1)} %bitcast.22) | data formatting | bytes 33554432
  17.7 0.0 copy-start.2
  17.7 0.0 copy-start.3
  17.7 273.0 %shard_map.103 = (bf16[768,1024]{1,0:T(8,128)(2,1)}, bf16[768,1024]{1,0:T(8,128)(2,1)}, bf16[64,768]{1,0:T(8,128)(2,1)}, bf16[64,768]{1,0:T(8,128)(2,1)}) custom-call(s32[4]{0:T(128)} %seg_tiles.1, s32[4]{0:T(128)} %seg_adapter.1, s32[16]{0:T(128)} %slot_of.1, bf16[768,1024]{1,0:T(8,128)(2,1)} %bitcast.28, bf16[768,1024]{1,0:T(8,128)(2,1)} %bitcast.29, ...), custom_call_target="tpu_custom_call" | custom-call | tf_op jit(solution)/shard_map/pallas_call | solution.py:268
  290.7 0.0 copy-done.2
  290.7 0.2 reduce-window.8
  290.9 0.1 convert_reduce_fusion
  291.0 0.0 copy-done.3
  291.0 0.1 select_reduce_fusion
  291.1 0.1 broadcast_bitcast_fusion
  291.2 0.0 copy-start.4
  291.2 1.3 broadcast_select_fusion
  292.4 0.2 copy-done.4
  292.7 0.0 copy-start.1
  292.7 3.8 %convolution_multiply_fusion = f32[1024,1024]{1,0:T(8,128)} fusion(bf16[1024,768]{1,0:T(8,128)(2,1)S(1)} %bitcast.27, bf16[768,1024]{1,0:T(8,128)(2,1)S(1)} %copy-done.4), kind=kOutput, calls=%fused_computation | convolution fusion | flops 1611661312 | bytes 7340032 | tf_op jit(solution)/shard_map/dot_general | solution.py:312
  296.5 0.0 copy-done.1
  296.5 0.0 copy-start
  296.5 3.8 %convolution_multiply_fusion.1 = f32[1024,1024]{1,0:T(8,128)} fusion(bf16[1024,768]{1,0:T(8,128)(2,1)S(1)} %bitcast.26, bf16[768,1024]{1,0:T(8,128)(2,1)S(1)} %bitcast.30), kind=kOutput, calls=%fused_computation.1 | convolution fusion | flops 1611661312 | bytes 7340032 | tf_op jit(solution)/shard_map/dot_general | solution.py:312
  300.3 0.0 copy-done
  300.3 1.1 copy.13
  (1 shorter events, 0.0 us)
Async XLA Ops:
  17.7 273.0 %copy-start.2 = (s32[4]{0:T(128)S(1)}, s32[4]{0:T(128)}, u32[]{:S(2)}) copy-start(s32[4]{0:T(128)} %seg_tiles.1) | copy-start | bytes 52
  17.7 273.3 %copy-start.3 = (s32[4]{0:T(128)S(1)}, s32[4]{0:T(128)}, u32[]{:S(2)}) copy-start(s32[4]{0:T(128)} %seg_adapter.1) | copy-start | bytes 52
  291.2 1.5 copy-start.4
  292.7 3.8 %copy-start.1 = (bf16[1,3,256,1024]{3,2,1,0:T(8,128)(2,1)S(1)}, bf16[1,3,256,1024]{3,2,1,0:T(8,128)(2,1)}, u32[]{:S(2)}) copy-start(bf16[1,3,256,1024]{3,2,1,0:T(8,128)(2,1)} %param.9) | copy-start | bytes 4718596
  296.5 3.8 %copy-start = (bf16[768,1024]{1,0:T(8,128)(2,1)S(1)}, bf16[768,1024]{1,0:T(8,128)(2,1)}, u32[]{:S(2)}) copy-start(bf16[768,1024]{1,0:T(8,128)(2,1)} %get-tuple-element.7) | copy-start | bytes 4718596

commit v2 on v1

--- a/solution.py
+++ b/solution.py
@@ -31,7 +31,7 @@
     grad_in, grad_own, low_u, low_h,
     w, gath, part, part_in, own_acc, sel_a, sel_b, put_a, put_b,
     u_part, u_pool, u_sum, u_all, h_part, h_pool, h_sum, h_all,
-    w_sem, g_send, g_recv, u_send, u_recv, up_send, up_recv, pp_send, pp_recv,
+    w_sem, g_send, g_down, g_recv, u_send, u_recv, up_send, up_recv, pp_send, pp_recv,
     sel_send, sel_recv, hp_send, hp_recv, h_send, h_recv, s_send, s_recv,
 ):
     n = lax.axis_size("tensor")
@@ -68,11 +68,27 @@
     def rows(k):
         return pl.ds(pl.multiple_of(k * TILE, TILE), TILE)
 
-    def gather_copy(k, sender, target):
-        place = gath.at[sender, rows(k)]
+    def block_copy(k, owner, target, sem):
+        place = gath.at[owner, rows(k)]
         return pltpu.make_async_remote_copy(
-            place, place, g_send.at[k, target], g_recv.at[k, sender],
+            place, place, sem, g_recv.at[k, owner],
             device_id={"tensor": target}, device_id_type=MESH)
+
+    def upward(k, owner):
+        return block_copy(k, owner, jnp.minimum(t + 1, n - 1), g_send.at[k, owner])
+
+    def downward(k, owner):
+        sem = g_send.at[k, owner] if owner is not t else g_down.at[k]
+        return block_copy(k, owner, jnp.maximum(t - 1, 0), sem)
+
+    def own_start(k):
+        @pl.when(t < n - 1)
+        def _():
+            upward(k, t).start()
+
+        @pl.when(t > 0)
+        def _():
+            downward(k, t).start()
 
     def u_copy(k, sender, target):
         return pltpu.make_async_remote_copy(
@@ -105,7 +121,7 @@
         gath[t] = cot[...]
 
         def first(k, _):
-            others(lambda tt: gather_copy(k, t, tt).start())
+            own_start(k)
             return 0
 
         lax.fori_loop(0, min(AHEAD, tiles), first, 0)
@@ -141,12 +157,10 @@
         @pl.when(s < top)
         def _():
             section_copy(k).wait_recv()
-            others(lambda tt: gather_copy(k, t, tt).start())
+            own_start(k)
 
         u_part[k] = row_dot(chosen(k, sel_b), gath[t, rows(k)])
         pool_copy(u_part.at[k], u_pool.at[k], up_send.at[k], up_recv.at[k]).start()
-
-    launch(0)
 
     def shrink_x(k, _):
         h_part[:, rows(k)] = row_dot(chosen(k, sel_a), x[rows(k)])
@@ -155,10 +169,15 @@
     lax.fori_loop(0, tiles, shrink_x, 0)
     h_pool_copy = pool_copy(h_part, h_pool, hp_send, hp_recv)
     h_pool_copy.start()
+    h_pool_copy.wait()
+    h_sum[...] = (h_part[...] + h_pool[...]).astype(BF16)
+
+    @pl.when(s < top)
+    def _():
+        others(lambda tt: h_copy(t, tt).start())
+
     w_copy.wait()
-    h_pool_copy.wait()
-    h_sum[...] = h_part[...] + h_pool[...]
-    others(lambda tt: h_copy(t, tt).start())
+    launch(0)
 
     def multiply(k, tt, half, acc, fresh):
         def one(b, _):
@@ -174,43 +193,69 @@
 
         lax.fori_loop(0, width // block, one, 0)
 
+    def arrive(k, d):
+        low, high = jnp.maximum(t - d, 0), jnp.minimum(t + d, n - 1)
+
+        @pl.when(t - d >= 0)
+        def _():
+            block_copy(k, low, low, g_send.at[k, low]).wait_recv()
+
+            @pl.when(t < n - 1)
+            def _():
+                upward(k, low).start()
+
+        @pl.when(t + d < n)
+        def _():
+            block_copy(k, high, high, g_send.at[k, high]).wait_recv()
+
+            @pl.when(t > 0)
+            def _():
+                downward(k, high).start()
+
+    def both(k, d, half, acc):
+        @pl.when(t - d >= 0)
+        def _():
+            multiply(k, jnp.maximum(t - d, 0), half, acc, False)
+
+        @pl.when(t + d < n)
+        def _():
+            multiply(k, jnp.minimum(t + d, n - 1), half, acc, False)
+
     def process(k, _):
-        @pl.when(k + 1 < tiles)
-        def _():
-            launch(k + 1)
-
         pool_copy(u_part.at[k], u_pool.at[k], up_send.at[k], up_recv.at[k]).wait()
-        u_sum[k] = u_part[k] + u_pool[k]
+        u_sum[k] = (u_part[k] + u_pool[k]).astype(BF16)
         others(lambda tt: u_copy(k, t, tt).start())
 
         send = part.at[k]
         multiply(k, t, q, send, True)
         multiply(k, t, p, own_acc, True)
 
-        def middle(i, _):
-            tt = lax.rem(t + i, n)
-            gather_copy(k, tt, tt).wait_recv()
-            multiply(k, tt, q, send, False)
-            multiply(k, tt, p, own_acc, False)
+        def middle(d, _):
+            arrive(k, d)
+            both(k, d, q, send)
+            both(k, d, p, own_acc)
             return 0
 
         lax.fori_loop(1, n - 1, middle, 0)
-        last = lax.rem(t + n - 1, n)
-        gather_copy(k, last, last).wait_recv()
 
         @pl.when((s == top) & (k + AHEAD < tiles))
         def _():
-            others(lambda tt: gather_copy(k + AHEAD, t, tt).start())
-
-        multiply(k, last, q, send, False)
+            own_start(k + AHEAD)
+
+        @pl.when(k + 1 < tiles)
+        def _():
+            launch(k + 1)
+
+        arrive(k, n - 1)
+        both(k, n - 1, q, send)
         half_copy = pool_copy(send, part_in.at[k], pp_send.at[k], pp_recv.at[k])
         half_copy.start()
-        multiply(k, last, p, own_acc, False)
+        both(k, n - 1, p, own_acc)
         u_all[k, t] = u_sum[k]
         others(lambda tt: u_copy(k, tt, tt).wait_recv())
-        u = u_all[k, 0]
+        u = u_all[k, 0].astype(F32)
         for i in range(1, n):
-            u = u + u_all[k, i]
+            u = u + u_all[k, i].astype(F32)
         low_u[:, rows(k)] = u.astype(BF16)
         expand = jnp.dot(u.T.astype(BF16), chosen(k, sel_a), preferred_element_type=F32)
         half_copy.wait()
@@ -224,25 +269,50 @@
 
     lax.fori_loop(0, tiles, process, 0)
 
+    @pl.when(s == top)
+    def _():
+        others(lambda tt: h_copy(t, tt).start())
+
     grad_own[...] = gath[t]
     h_all[t] = h_sum[...]
     others(lambda tt: h_copy(tt, tt).wait_recv())
-    h = h_all[0]
+    h = h_all[0].astype(F32)
     for i in range(1, n):
-        h = h + h_all[i]
+        h = h + h_all[i].astype(F32)
     low_h[...] = h.astype(BF16)
 
     def sent(tt):
         h_copy(t, tt).wait_send()
 
         def one(k, _):
-            gather_copy(k, t, tt).wait_send()
             u_copy(k, t, tt).wait_send()
+
+            @pl.when((tt < t) & (t < n - 1))
+            def _():
+                upward(k, tt).wait_send()
+
+            @pl.when((tt > t) & (t > 0))
+            def _():
+                downward(k, tt).wait_send()
+
             return 0
 
         lax.fori_loop(0, tiles, one, 0)
 
     others(sent)
+
+    def own_sent(k, _):
+        @pl.when(t < n - 1)
+        def _():
+            upward(k, t).wait_send()
+
+        @pl.when(t > 0)
+        def _():
+            downward(k, t).wait_send()
+
+        return 0
+
+    lax.fori_loop(0, tiles, own_sent, 0)
 
     @pl.when(s > 0)
     def _():
@@ -287,14 +357,14 @@
             pltpu.VMEM((segs, rank, width), BF16),
             pltpu.VMEM((tiles, rank, TILE), F32),
             pltpu.VMEM((tiles, rank, TILE), F32),
-            pltpu.VMEM((tiles, rank, TILE), F32),
-            pltpu.VMEM((tiles, n, rank, TILE), F32),
+            pltpu.VMEM((tiles, rank, TILE), BF16),
+            pltpu.VMEM((tiles, n, rank, TILE), BF16),
             pltpu.VMEM((rank, m), F32),
             pltpu.VMEM((rank, m), F32),
-            pltpu.VMEM((rank, m), F32),
-            pltpu.VMEM((n, rank, m), F32),
+            pltpu.VMEM((rank, m), BF16),
+            pltpu.VMEM((n, rank, m), BF16),
             dma(()),
-            dma((tiles, n)), dma((tiles, n)), dma((tiles, n)), dma((tiles, n)),
+            dma((tiles, n)), dma((tiles,)), dma((tiles, n)), dma((tiles, n)), dma((tiles, n)),
             dma((tiles,)), dma((tiles,)), dma((tiles,)), dma((tiles,)),
             dma((2,)), dma((2,)), dma(()), dma(()), dma((n,)), dma((n,)),
             dma((tiles,)), dma((tiles,)),

time: 302 us -> 193 us (0.64)
  Pallas kernels: 273 us -> 165 us
    pallas_call x1, Pallas kernels: 273 us -> 165 us  [per_device(): pl.pallas_call(kernel, out_shape=(jax.ShapeDtypeStruct((m, width), BF16),...]
where the time goes in v2:
time: 193 us
  Pallas kernels  165 us (85%)
  local copies, waits for them, and re-layouts  18.5 us (10%)
  matrix products  7.61 us (4%)
    pallas_call x1, Pallas kernels, per_device(): pl.pallas_call(kernel, out_shape=(jax.ShapeDtypeStruct((m, width), BF16),...  165 us
    unnamed x12, local copies, waits for them, and re-layouts  18.4 us
    dot_general x2, matrix products, spread(): full = SCALE * jnp.dot(lanes, wide, preferred_element_type=F32)  7.61 us

profile of v2, /device:TPU:0, one launch (start us, length us, event | category | flops | bytes accessed | tf_op | source)
XLA Modules:
  0.0 192.9 jit_solution(1251322142491446068)
XLA Ops:
  0.6 17.0 %copy.11 = bf16[256,8,4,1024]{3,1,2,0:T(8,128)(2,1)} copy(bf16[256,8,4,1024]{3,2,1,0:T(4,128)(2,1)} %bitcast.22) | data formatting | bytes 33554432
  17.7 0.0 copy-start.2
  17.7 0.0 copy-start.3
  17.7 164.5 %shard_map.103 = (bf16[768,1024]{1,0:T(8,128)(2,1)}, bf16[768,1024]{1,0:T(8,128)(2,1)}, bf16[64,768]{1,0:T(8,128)(2,1)}, bf16[64,768]{1,0:T(8,128)(2,1)}) custom-call(s32[4]{0:T(128)} %seg_tiles.1, s32[4]{0:T(128)} %seg_adapter.1, s32[16]{0:T(128)} %slot_of.1, bf16[768,1024]{1,0:T(8,128)(2,1)} %bitcast.28, bf16[768,1024]{1,0:T(8,128)(2,1)} %bitcast.29, ...), custom_call_target="tpu_custom_call" | custom-call | tf_op jit(solution)/shard_map/pallas_call | solution.py:338
  182.2 0.0 copy-done.2
  182.2 0.2 reduce-window.8
  182.4 0.1 convert_reduce_fusion
  182.4 0.0 copy-done.3
  182.5 0.1 select_reduce_fusion
  182.5 0.1 broadcast_bitcast_fusion
  182.6 0.0 copy-start.4
  182.6 1.3 broadcast_select_fusion
  183.9 0.2 copy-done.4
  184.1 0.0 copy-start.1
  184.1 3.8 %convolution_multiply_fusion = f32[1024,1024]{1,0:T(8,128)} fusion(bf16[1024,768]{1,0:T(8,128)(2,1)S(1)} %bitcast.27, bf16[768,1024]{1,0:T(8,128)(2,1)S(1)} %copy-done.4), kind=kOutput, calls=%fused_computation | convolution fusion | flops 1611661312 | bytes 7340032 | tf_op jit(solution)/shard_map/dot_general | solution.py:382
  187.9 0.0 copy-done.1
  187.9 0.0 copy-start
  187.9 3.8 %convolution_multiply_fusion.1 = f32[1024,1024]{1,0:T(8,128)} fusion(bf16[1024,768]{1,0:T(8,128)(2,1)S(1)} %bitcast.26, bf16[768,1024]{1,0:T(8,128)(2,1)S(1)} %bitcast.30), kind=kOutput, calls=%fused_computation.1 | convolution fusion | flops 1611661312 | bytes 7340032 | tf_op jit(solution)/shard_map/dot_general | solution.py:382
  191.8 0.0 copy-done
  191.8 1.1 copy.13
  (1 shorter events, 0.0 us)
Async XLA Ops:
  17.7 164.5 %copy-start.2 = (s32[4]{0:T(128)S(1)}, s32[4]{0:T(128)}, u32[]{:S(2)}) copy-start(s32[4]{0:T(128)} %seg_tiles.1) | copy-start | bytes 52
  17.7 164.8 %copy-start.3 = (s32[4]{0:T(128)S(1)}, s32[4]{0:T(128)}, u32[]{:S(2)}) copy-start(s32[4]{0:T(128)} %seg_adapter.1) | copy-start | bytes 52
  182.6 1.5 copy-start.4
  184.1 3.8 %copy-start.1 = (bf16[1,3,256,1024]{3,2,1,0:T(8,128)(2,1)S(1)}, bf16[1,3,256,1024]{3,2,1,0:T(8,128)(2,1)}, u32[]{:S(2)}) copy-start(bf16[1,3,256,1024]{3,2,1,0:T(8,128)(2,1)} %param.9) | copy-start | bytes 4718596
  187.9 3.8 %copy-start = (bf16[768,1024]{1,0:T(8,128)(2,1)S(1)}, bf16[768,1024]{1,0:T(8,128)(2,1)}, u32[]{:S(2)}) copy-start(bf16[768,1024]{1,0:T(8,128)(2,1)} %get-tuple-element.7) | copy-start | bytes 4718596

commit v3 on v2

--- a/solution.py
+++ b/solution.py
@@ -29,7 +29,7 @@
 def kernel(
     seg_tiles, seg_adapter, slot_of, cot, x, w_hbm, panel_a, panel_b,
     grad_in, grad_own, low_u, low_h,
-    w, gath, part, part_in, own_acc, sel_a, sel_b, put_a, put_b,
+    w, w_raw, gath, part, part_in, own_acc, sel_a, sel_b, put_a, put_b,
     u_part, u_pool, u_sum, u_all, h_part, h_pool, h_sum, h_all,
     w_sem, g_send, g_down, g_recv, u_send, u_recv, up_send, up_recv, pp_send, pp_recv,
     sel_send, sel_recv, hp_send, hp_recv, h_send, h_recv, s_send, s_recv,
@@ -61,8 +61,14 @@
     def _():
         pl.semaphore_signal(barrier, inc=1, device_id={"section": s + 1}, device_id_type=MESH)
 
-    w_copy = pltpu.make_async_copy(w_hbm, w, w_sem)
-    w_copy.start()
+    parts = w_hbm.shape[0] // block
+
+    def w_copy(b):
+        slot = lax.rem(b, 2)
+        source = w_hbm.at[pl.ds(pl.multiple_of(b * block, block), block)]
+        return pltpu.make_async_copy(source, w_raw.at[slot], w_sem.at[slot])
+
+    w_copy(jnp.int32(0)).start()
     pl.semaphore_wait(barrier, n + (s > 0).astype(jnp.int32) + (s < top).astype(jnp.int32))
 
     def rows(k):
@@ -176,7 +182,26 @@
     def _():
         others(lambda tt: h_copy(t, tt).start())
 
-    w_copy.wait()
+    def unpack(b, _):
+        @pl.when(b + 1 < parts)
+        def _():
+            w_copy(b + 1).start()
+
+        w_copy(b).wait()
+        raw = w_raw.at[lax.rem(b, 2)]
+        step = min(64, block)
+
+        def rows_of(i, _):
+            r = pl.multiple_of(i * step, step)
+            piece = raw[pl.ds(r, step)].astype(F32)
+            for tt in range(n):
+                w[pl.ds(pl.multiple_of(b * block + r, step), step), tt * width:(tt + 1) * width] = piece[:, tt].astype(BF16)
+            return 0
+
+        lax.fori_loop(0, block // step, rows_of, 0)
+        return 0
+
+    lax.fori_loop(0, parts, unpack, 0)
     launch(0)
 
     def multiply(k, tt, half, acc, fresh):
@@ -328,7 +353,7 @@
     micro, row_count, width = cotangent.shape
     m = micro * row_count
     tiles = m // TILE
-    weight = base_weight[0].reshape(base_weight.shape[1], -1)
+    weight = base_weight[0].reshape(base_weight.shape[1], n, width)
     x = saved_inputs[0].reshape(m, width)
     rank = panel_a.shape[2]
     segs = seg_tiles.shape[0]
@@ -346,7 +371,8 @@
         in_specs=[smem] * 3 + [vmem] * 2 + [pl.BlockSpec(memory_space=pl.ANY)] + [vmem] * 2,
         out_specs=(vmem,) * 4,
         scratch_shapes=[
-            pltpu.VMEM(weight.shape, BF16),
+            pltpu.VMEM((weight.shape[0], n * width), BF16),
+            pltpu.VMEM((2, min(256, width), n, width), BF16),
             pltpu.VMEM((n, m, width), BF16),
             pltpu.VMEM((tiles, TILE, width), F32),
             pltpu.VMEM((tiles, TILE, width), F32),
@@ -363,7 +389,7 @@
             pltpu.VMEM((rank, m), F32),
             pltpu.VMEM((rank, m), BF16),
             pltpu.VMEM((n, rank, m), BF16),
-            dma(()),
+            dma((2,)),
             dma((tiles, n)), dma((tiles,)), dma((tiles, n)), dma((tiles, n)), dma((tiles, n)),
             dma((tiles,)), dma((tiles,)), dma((tiles,)), dma((tiles,)),
             dma((2,)), dma((2,)), dma(()), dma(()), dma((n,)), dma((n,)),

time: 193 us -> 216 us (1.12)
  Pallas kernels: 165 us -> 204 us
  local copies, waits for them, and re-layouts: 18.5 us -> 1.44 us
    pallas_call x1, Pallas kernels: 165 us -> 204 us  [per_device(): pl.pallas_call(kernel, out_shape=(jax.ShapeDtypeStruct((m, width), BF16),...]
    unnamed x12 -> x7, local copies, waits for them, and re-layouts: 18.4 us -> 1.37 us
where the time goes in v3:
time: 216 us
  Pallas kernels  204 us (94%)
  matrix products  7.61 us (4%)
  other arithmetic  2.95 us (1%)
    pallas_call x1, Pallas kernels, per_device(): pl.pallas_call(kernel, out_shape=(jax.ShapeDtypeStruct((m, width), BF16),...  204 us
    dot_general x2, matrix products, spread(): full = SCALE * jnp.dot(lanes, wide, preferred_element_type=F32)  7.61 us

profile of v3, /device:TPU:0, one launch (start us, length us, event | category | flops | bytes accessed | tf_op | source)
XLA Modules:
  0.0 216.3 jit_solution(14860032902385299403)
XLA Ops:
  0.6 0.8 reduce-window.8
  1.5 0.1 convert_reduce_fusion
  1.5 0.7 select_reduce_fusion
  2.3 0.1 broadcast_bitcast_fusion
  2.4 203.7 %shard_map.103 = (bf16[768,1024]{1,0:T(8,128)(2,1)}, bf16[768,1024]{1,0:T(8,128)(2,1)}, bf16[64,768]{1,0:T(8,128)(2,1)}, bf16[64,768]{1,0:T(8,128)(2,1)}) custom-call(s32[4]{0:T(128)} %seg_tiles.1, s32[4]{0:T(128)} %seg_adapter.1, s32[16]{0:T(128)} %slot_of.1, bf16[768,1024]{1,0:T(8,128)(2,1)} %bitcast.24, bf16[768,1024]{1,0:T(8,128)(2,1)} %bitcast.25, ...), custom_call_target="tpu_custom_call" | custom-call | tf_op jit(solution)/shard_map/pallas_call | solution.py:363
  206.0 0.0 copy-start.2
  206.0 1.3 broadcast_select_fusion
  207.3 0.2 copy-done.2
  207.5 0.0 copy-start.1
  207.5 3.8 %convolution_multiply_fusion = f32[1024,1024]{1,0:T(8,128)} fusion(bf16[1024,768]{1,0:T(8,128)(2,1)S(1)} %bitcast.23, bf16[768,1024]{1,0:T(8,128)(2,1)S(1)} %copy-done.2), kind=kOutput, calls=%fused_computation | convolution fusion | flops 1611661312 | bytes 7340032 | tf_op jit(solution)/shard_map/dot_general | solution.py:408
  211.4 0.0 copy-done.1
  211.4 0.0 copy-start
  211.4 3.8 %convolution_multiply_fusion.1 = f32[1024,1024]{1,0:T(8,128)} fusion(bf16[1024,768]{1,0:T(8,128)(2,1)S(1)} %bitcast.22, bf16[768,1024]{1,0:T(8,128)(2,1)S(1)} %bitcast.26), kind=kOutput, calls=%fused_computation.1 | convolution fusion | flops 1611661312 | bytes 7340032 | tf_op jit(solution)/shard_map/dot_general | solution.py:408
  215.2 0.0 copy-done
  215.2 1.1 copy.12
  (1 shorter events, 0.0 us)
Async XLA Ops:
  206.0 1.5 copy-start.2
  207.5 3.8 %copy-start.1 = (bf16[1,3,256,1024]{3,2,1,0:T(8,128)(2,1)S(1)}, bf16[1,3,256,1024]{3,2,1,0:T(8,128)(2,1)}, u32[]{:S(2)}) copy-start(bf16[1,3,256,1024]{3,2,1,0:T(8,128)(2,1)} %param.9) | copy-start | bytes 4718596
  211.4 3.8 %copy-start = (bf16[768,1024]{1,0:T(8,128)(2,1)S(1)}, bf16[768,1024]{1,0:T(8,128)(2,1)}, u32[]{:S(2)}) copy-start(bf16[768,1024]{1,0:T(8,128)(2,1)} %get-tuple-element.7) | copy-start | bytes 4718596
